TPU v7x, 256 devices: a whole 4x4x8 slice. The times are simulated.
256 devices in a mesh: seq: 32 (over y, z_lo, core), dp: 8 (over z_hi, x).
Axes of the slice: x: 4, y: 4, z: 8 (z_hi: 2, z_lo: 4; z = z_hi * 4 + z_lo), core: 2. Of those that a mesh axis runs over, the one named last changes fastest.
Arguments:
- query_rows: bfloat16 [16, 2048, 4096], P('dp', 'seq'), as said below
- key_rows: bfloat16 [16, 2048, 4096], P('dp', 'seq'), as said below
- value_rows: bfloat16 [16, 2048, 4096], P('dp', 'seq'), may hold values from -6 to 6
- query_tangent: bfloat16 [16, 2048, 4096], P('dp', 'seq'), may hold values from -6 to 6
- key_tangent: bfloat16 [16, 2048, 4096], P('dp', 'seq'), may hold values from -6 to 6
- value_tangent: bfloat16 [16, 2048, 4096], P('dp', 'seq'), may hold values from -6 to 6
- query_gain: float32 [4096], P('dp'), may hold values from 0.5 to 1.5
- key_gain: float32 [4096], P('dp'), may hold values from 0.5 to 1.5
Outputs:
- attended: bfloat16 [16, 2048, 4096], P('dp', 'seq')
- attended_tangent: bfloat16 [16, 2048, 4096], P('dp', 'seq')
Inputs may be any that keep to these rules, and one draw needn't show every extreme that they name: `query_rows`: entries lie within -160 and 160. `key_rows`: entries lie within -160 and 160.
All inputs are finite; a program needn't handle non-finite values.
Results may differ from a plain program's by a relative error of at most 0.012.
The roundings to bfloat16 on the way count: a program that leaves them out, or rounds other values in their place, can miss the bound.
Values may be sent and summed in bfloat16 or wider, within the bound.
A program may use at most 64 MiB of HBM per device.

v0:
```python
import jax
import jax.numpy as jnp
from jax import lax
from jax.sharding import PartitionSpec as P

HEADS = 32


EPS = 1e-06


def normalize(rows, tangent, gain):
    xf = rows.astype(jnp.float32)
    dxf = tangent.astype(jnp.float32)
    inverse = lax.rsqrt(jnp.mean(xf * xf, axis=-1, keepdims=True) + EPS)
    cross = jnp.mean(xf * dxf, axis=-1, keepdims=True)
    normed = xf * inverse * gain
    dnormed = (dxf * inverse - xf * inverse**3 * cross) * gain
    return (normed.astype(jnp.bfloat16), dnormed.astype(jnp.bfloat16))


def head_attention(parts):
    qh, kh, vh, dqh, dkh, dvh = parts
    length, hdim = qh.shape
    block = min(512, length)
    scale = hdim ** (-0.5)

    def one_block(pair):
        qblock, dqblock = pair
        scores = jnp.dot(qblock, kh.T, preferred_element_type=jnp.float32) * scale
        top = jnp.max(scores, axis=-1, keepdims=True)
        weights = jnp.exp(scores - top)
        weights = weights / jnp.sum(weights, axis=-1, keepdims=True)
        tangent = (
            jnp.dot(dqblock, kh.T, preferred_element_type=jnp.float32)
            + jnp.dot(qblock, dkh.T, preferred_element_type=jnp.float32)
        ) * scale
        dweights = weights * (tangent - jnp.sum(weights * tangent, axis=-1, keepdims=True))
        weights_low = weights.astype(jnp.bfloat16)
        tangent_low = dweights.astype(jnp.bfloat16)
        output = jnp.dot(weights_low, vh, preferred_element_type=jnp.float32).astype(jnp.bfloat16)
        doutput = (
            jnp.dot(tangent_low, vh, preferred_element_type=jnp.float32)
            + jnp.dot(weights_low, dvh, preferred_element_type=jnp.float32)
        ).astype(jnp.bfloat16)
        return (output, doutput)

    blocks = length // block
    output, doutput = lax.map(
        one_block, (qh.reshape(blocks, block, hdim), dqh.reshape(blocks, block, hdim))
    )
    return (output.reshape(length, hdim), doutput.reshape(length, hdim))


def attend_all(parts):
    clips_here, length, local_heads, hdim = parts[0].shape

    def flatten(array):
        return array.transpose(0, 2, 1, 3).reshape(clips_here * local_heads, length, hdim)

    def unflatten(array):
        return array.reshape(clips_here, local_heads, length, hdim).transpose(0, 2, 1, 3)

    output, doutput = lax.map(head_attention, tuple((flatten(array) for array in parts)))
    return (unflatten(output), unflatten(doutput))


def on_device(
    query_rows,
    key_rows,
    value_rows,
    query_tangent,
    key_tangent,
    value_tangent,
    query_gain,
    key_gain,
):
    full_query_gain, full_key_gain = (
        lax.all_gather(query_gain, "dp", axis=0, tiled=True),
        lax.all_gather(key_gain, "dp", axis=0, tiled=True),
    )
    qn, dqn = normalize(query_rows, query_tangent, full_query_gain)
    kn, dkn = normalize(key_rows, key_tangent, full_key_gain)
    clips_here, tok_rows, width_here = query_rows.shape

    def split(array):
        return array.reshape(clips_here, tok_rows, HEADS, width_here // HEADS)

    head_query, head_key, head_value = (
        lax.all_to_all(split(qn), "seq", split_axis=2, concat_axis=1, tiled=True),
        lax.all_to_all(split(kn), "seq", split_axis=2, concat_axis=1, tiled=True),
        lax.all_to_all(split(value_rows), "seq", split_axis=2, concat_axis=1, tiled=True),
    )
    head_dquery, head_dkey, head_dvalue = (
        lax.all_to_all(split(dqn), "seq", split_axis=2, concat_axis=1, tiled=True),
        lax.all_to_all(split(dkn), "seq", split_axis=2, concat_axis=1, tiled=True),
        lax.all_to_all(split(value_tangent), "seq", split_axis=2, concat_axis=1, tiled=True),
    )
    attended, attended_tangent = attend_all(
        (head_query, head_key, head_value, head_dquery, head_dkey, head_dvalue)
    )
    attended = lax.all_to_all(attended, "seq", split_axis=1, concat_axis=2, tiled=True)
    attended_tangent = lax.all_to_all(
        attended_tangent, "seq", split_axis=1, concat_axis=2, tiled=True
    )
    return (
        attended.reshape(clips_here, tok_rows, width_here),
        attended_tangent.reshape(clips_here, tok_rows, width_here),
    )


def solution(mesh):
    return jax.shard_map(
        on_device,
        mesh=mesh,
        in_specs=(
            P("dp", "seq", None),
            P("dp", "seq", None),
            P("dp", "seq", None),
            P("dp", "seq", None),
            P("dp", "seq", None),
            P("dp", "seq", None),
            P("dp"),
            P("dp"),
        ),
        out_specs=(P("dp", "seq", None), P("dp", "seq", None)),
        check_vma=False,
    )
```

profile of v0, /device:TPU:1, one launch (start us, length us, event | category | flops | bytes accessed | tf_op | source)
XLA Modules:
  0.0 433.7 jit_solution(17888934505845071413)
XLA Ops:
  0.7 37.9 %all-gather = f32[8,1,512]{2,1,0:T(1,128)S(1)} all-gather(f32[1,1,512]{2,1,0:T(1,128)} %bitcast.177), channel_id=1, replica_groups=mesh['seq'=32,'dp'=8] {'dp'}, dimensions={0}, use_global_device_ids=true | all-gather | bytes 18432 | tf_op jit(solution)/shard_map/all_gather | solution.py:79
  42.8 11.8 %all-to-all-start = ((bf16[2,64,32,128]{3,1,0,2:T(8,128)(2,1)}), bf16[2,64,32,128]{3,1,0,2:T(8,128)(2,1)S(1)}, u32[]{:S(2)}, u32[]{:S(2)}) async-start(bf16[2,64,32,128]{3,1,0,2:T(8,128)(2,1)} %bitcast.122), calls=%async_computation | async-start | bytes 2097152 | tf_op jit(solution)/shard_map/all_to_all | solution.py:90
  55.9 26.6 %all-to-all-done = bf16[2,64,32,128]{3,1,0,2:T(8,128)(2,1)S(1)} async-done(((bf16[2,64,32,128]{3,1,0,2:T(8,128)(2,1)}), bf16[2,64,32,128]{3,1,0,2:T(8,128)(2,1)S(1)}, u32[]{:S(2)}, u32[]{:S(2)}) %all-to-all-start) | async-done | bytes 1048608 | tf_op jit(solution)/shard_map/all_to_all | solution.py:90
  82.5 3.9 all-to-all-start.1
  86.4 48.0 %all-gather.1 = f32[8,1,512]{2,1,0:T(1,128)S(1)} all-gather(f32[1,1,512]{2,1,0:T(1,128)S(1)} %bitcast.178), channel_id=1, replica_groups=mesh['seq'=32,'dp'=8] {'dp'}, dimensions={0}, use_global_device_ids=true | all-gather | bytes 18432 | tf_op jit(solution)/shard_map/all_gather | solution.py:80
  139.7 12.0 %all-to-all-start.2 = ((bf16[2,64,32,128]{3,1,0,2:T(8,128)(2,1)}), bf16[2,64,32,128]{3,1,0,2:T(8,128)(2,1)}, u32[]{:S(2)}, u32[]{:S(2)}) async-start(bf16[2,64,32,128]{3,1,0,2:T(8,128)(2,1)} %bitcast.172), calls=%async_computation.2 | async-start | bytes 2097152 | tf_op jit(solution)/shard_map/all_to_all | solution.py:91
  151.7 2.5 copy.52
  154.2 25.4 %all-to-all-done.2 = bf16[2,64,32,128]{3,1,0,2:T(8,128)(2,1)} async-done(((bf16[2,64,32,128]{3,1,0,2:T(8,128)(2,1)}), bf16[2,64,32,128]{3,1,0,2:T(8,128)(2,1)}, u32[]{:S(2)}, u32[]{:S(2)}) %all-to-all-start.2) | async-done | bytes 1048608 | tf_op jit(solution)/shard_map/all_to_all | solution.py:91
  179.6 3.9 all-to-all-start.3
  184.8 26.7 %all-to-all-done.3 = bf16[2,64,32,128]{3,1,0,2:T(8,128)(2,1)S(1)} async-done(((bf16[2,64,32,128]{3,1,0,2:T(8,128)(2,1)}), bf16[2,64,32,128]{3,1,0,2:T(8,128)(2,1)S(1)}, u32[]{:S(2)}, u32[]{:S(2)}) %all-to-all-start.3) | async-done | bytes 1048608 | tf_op jit(solution)/shard_map/all_to_all | solution.py:96
  211.5 4.6 %all-to-all-start.4 = ((bf16[2,64,32,128]{3,1,0,2:T(8,128)(2,1)}), bf16[2,64,32,128]{3,1,0,2:T(8,128)(2,1)}, u32[]{:S(2)}, u32[]{:S(2)}) async-start(bf16[2,64,32,128]{3,1,0,2:T(8,128)(2,1)} %copy_bitcast_fusion.1), calls=%async_computation.4 | async-start | bytes 2097152 | tf_op jit(solution)/shard_map/all_to_all | solution.py:92
  216.1 2.5 copy_bitcast_fusion
  218.6 25.5 %all-to-all-done.4 = bf16[2,64,32,128]{3,1,0,2:T(8,128)(2,1)} async-done(((bf16[2,64,32,128]{3,1,0,2:T(8,128)(2,1)}), bf16[2,64,32,128]{3,1,0,2:T(8,128)(2,1)}, u32[]{:S(2)}, u32[]{:S(2)}) %all-to-all-start.4) | async-done | bytes 1048608 | tf_op jit(solution)/shard_map/all_to_all | solution.py:92
  244.1 4.6 %all-to-all-start.5 = ((bf16[2,64,32,128]{3,1,0,2:T(8,128)(2,1)}), bf16[2,64,32,128]{3,1,0,2:T(8,128)(2,1)}, u32[]{:S(2)}, u32[]{:S(2)}) async-start(bf16[2,64,32,128]{3,1,0,2:T(8,128)(2,1)} %copy_bitcast_fusion), calls=%async_computation.5 | async-start | bytes 2097152 | tf_op jit(solution)/shard_map/all_to_all | solution.py:97
  256.9 19.9 %all-to-all-done.5 = bf16[2,64,32,128]{3,1,0,2:T(8,128)(2,1)} async-done(((bf16[2,64,32,128]{3,1,0,2:T(8,128)(2,1)}), bf16[2,64,32,128]{3,1,0,2:T(8,128)(2,1)}, u32[]{:S(2)}, u32[]{:S(2)}) %all-to-all-start.5) | async-done | bytes 1048608 | tf_op jit(solution)/shard_map/all_to_all | solution.py:97
  279.0 85.2 %while.25 = (s32[]{:T(128)}, bf16[2,2048,128]{2,1,0:T(8,128)(2,1)}, bf16[2,2048,128]{2,1,0:T(8,128)(2,1)}, bf16[2,2048,128]{2,1,0:T(8,128)(2,1)S(1)}, bf16[2,204...) while((s32[]{:T(128)}, bf16[2,2048,128]{2,1,0:T(8,128)(2,1)}, ...), condition=%wide.region_10.11_spmd, body=%wide.region_4.10_spmd.sunk | while | flops 1628633600 | bytes 86131216 | solution.py:64
  282.4 36.9 %while.26 = (s32[]{:T(128)}, bf16[4,512,128]{2,1,0:T(8,128)(2,1)}, bf16[4,512,128]{2,1,0:T(8,128)(2,1)}, bf16[4,512,128]{2,1,0:T(8,128)(2,1)S(1)}, bf16[2048,128...) while((s32[]{:T(128)}, bf16[4,512,128]{2,1,0:T(8,128)(2,1)}, ...), condition=%wide.region_9.9_spmd, body=%wide.region_5.8_spmd.sunk | while | flops 1628633600 | bytes 52575880 | solution.py:49
  325.0 36.9 %while.26 = (s32[]{:T(128)}, bf16[4,512,128]{2,1,0:T(8,128)(2,1)}, bf16[4,512,128]{2,1,0:T(8,128)(2,1)}, bf16[4,512,128]{2,1,0:T(8,128)(2,1)S(1)}, bf16[2048,128...) while((s32[]{:T(128)}, bf16[4,512,128]{2,1,0:T(8,128)(2,1)}, ...), condition=%wide.region_9.9_spmd, body=%wide.region_5.8_spmd.sunk | while | flops 1628633600 | bytes 52575880 | solution.py:49
  364.2 3.7 copy.57
  367.9 3.9 all-to-all-start.6
  371.8 9.5 %copy.56 = bf16[2,2048,128]{2,0,1:T(2,128)(2,1)} copy(bf16[2,2048,128]{2,1,0:T(8,128)(2,1)S(1)} %copy-done.15) | data formatting | bytes 2097152 | tf_op jit(solution)/shard_map/while | solution.py:64
  381.3 18.5 %all-to-all-done.6 = bf16[2,2048,1,128]{3,0,2,1:T(2,128)(2,1)S(1)} async-done(((bf16[2,2048,1,128]{3,0,2,1:T(2,128)(2,1)}), bf16[2,2048,1,128]{3,0,2,1:T(2,128)(2,1)S(1)}, u32[]{:S(2)}, u32[]{:S(2)}) %all-to-all-start.6) | async-done | bytes 1048608 | tf_op jit(solution)/shard_map/all_to_all | solution.py:102
  399.8 3.9 all-to-all-start.7
  407.7 24.0 %all-to-all-done.7 = bf16[2,2048,1,128]{3,0,2,1:T(2,128)(2,1)S(1)} async-done(((bf16[2,2048,1,128]{3,0,2,1:T(2,128)(2,1)}), bf16[2,2048,1,128]{3,0,2,1:T(2,128)(2,1)S(1)}, u32[]{:S(2)}, u32[]{:S(2)}) %all-to-all-start.7) | async-done | bytes 1048608 | tf_op jit(solution)/shard_map/all_to_all | solution.py:103
  (157 shorter events, 112.9 us)
Async XLA Ops:
  0.6 182.9 %copy-start = (bf16[2,64,4096]{2,1,0:T(8,128)(2,1)S(1)}, bf16[2,64,4096]{2,1,0:T(8,128)(2,1)}, u32[]{:S(2)}) copy-start(bf16[2,64,4096]{2,1,0:T(8,128)(2,1)} %param.14) | copy-start | bytes 3145732
  0.6 40.0 %copy-start.11 = (bf16[2,64,4096]{2,1,0:T(8,128)(2,1)S(1)}, bf16[2,64,4096]{2,1,0:T(8,128)(2,1)}, u32[]{:S(2)}) copy-start(bf16[2,64,4096]{2,1,0:T(8,128)(2,1)} %param.12) | copy-start | bytes 3145732
  0.7 40.0 %copy-start.12 = (bf16[2,64,4096]{2,1,0:T(8,128)(2,1)S(1)}, bf16[2,64,4096]{2,1,0:T(8,128)(2,1)}, u32[]{:S(2)}) copy-start(bf16[2,64,4096]{2,1,0:T(8,128)(2,1)} %param.15) | copy-start | bytes 3145732
  42.8 39.7 %all-to-all-start = ((bf16[2,64,32,128]{3,1,0,2:T(8,128)(2,1)}), bf16[2,64,32,128]{3,1,0,2:T(8,128)(2,1)S(1)}, u32[]{:S(2)}, u32[]{:S(2)}) async-start(bf16[2,64,32,128]{3,1,0,2:T(8,128)(2,1)} %bitcast.122), calls=%async_computation | async-start | bytes 2097152 | tf_op jit(solution)/shard_map/all_to_all | solution.py:90
  54.6 31.8 %copy-start.16 = (f32[512]{0:T(512)S(1)}, f32[512]{0:T(512)}, u32[]{:S(2)}) copy-start(f32[512]{0:T(512)} %param.19) | copy-start | bytes 6148
  82.5 57.2 %all-to-all-start.1 = ((bf16[2,64,32,128]{3,1,0,2:T(8,128)(2,1)}), bf16[2,64,32,128]{3,1,0,2:T(8,128)(2,1)S(1)}, u32[]{:S(2)}, u32[]{:S(2)}) async-start(bf16[2,64,32,128]{3,1,0,2:T(8,128)(2,1)} %bitcast.170), calls=%async_computation.1 | async-start | bytes 2097152 | tf_op jit(solution)/shard_map/all_to_all | solution.py:95
  86.4 50.1 %copy-start.13 = (bf16[2,64,4096]{2,1,0:T(8,128)(2,1)S(1)}, bf16[2,64,4096]{2,1,0:T(8,128)(2,1)}, u32[]{:S(2)}) copy-start(bf16[2,64,4096]{2,1,0:T(8,128)(2,1)} %param.13) | copy-start | bytes 3145732
  86.4 50.1 %copy-start.14 = (bf16[2,64,4096]{2,1,0:T(8,128)(2,1)S(1)}, bf16[2,64,4096]{2,1,0:T(8,128)(2,1)}, u32[]{:S(2)}) copy-start(bf16[2,64,4096]{2,1,0:T(8,128)(2,1)} %param.16) | copy-start | bytes 3145732
  139.7 14.5 %copy-start.8 = (bf16[2,64,32,128]{3,1,0,2:T(8,128)(2,1)}, bf16[2,64,32,128]{3,1,0,2:T(8,128)(2,1)S(1)}, u32[]{:S(2)}) copy-start(bf16[2,64,32,128]{3,1,0,2:T(8,128)(2,1)S(1)} %all-to-all-done.1) | copy-start | bytes 3145732
  139.7 39.9 %all-to-all-start.2 = ((bf16[2,64,32,128]{3,1,0,2:T(8,128)(2,1)}), bf16[2,64,32,128]{3,1,0,2:T(8,128)(2,1)}, u32[]{:S(2)}, u32[]{:S(2)}) async-start(bf16[2,64,32,128]{3,1,0,2:T(8,128)(2,1)} %bitcast.172), calls=%async_computation.2 | async-start | bytes 2097152 | tf_op jit(solution)/shard_map/all_to_all | solution.py:91
  179.6 31.9 %all-to-all-start.3 = ((bf16[2,64,32,128]{3,1,0,2:T(8,128)(2,1)}), bf16[2,64,32,128]{3,1,0,2:T(8,128)(2,1)S(1)}, u32[]{:S(2)}, u32[]{:S(2)}) async-start(bf16[2,64,32,128]{3,1,0,2:T(8,128)(2,1)} %bitcast.174), calls=%async_computation.3 | async-start | bytes 2097152 | tf_op jit(solution)/shard_map/all_to_all | solution.py:96
  211.5 7.1 %copy-start.9 = (bf16[2,64,32,128]{3,1,0,2:T(8,128)(2,1)}, bf16[2,64,32,128]{3,1,0,2:T(8,128)(2,1)S(1)}, u32[]{:S(2)}) copy-start(bf16[2,64,32,128]{3,1,0,2:T(8,128)(2,1)S(1)} %all-to-all-done.3) | copy-start | bytes 3145732
  211.5 32.6 %all-to-all-start.4 = ((bf16[2,64,32,128]{3,1,0,2:T(8,128)(2,1)}), bf16[2,64,32,128]{3,1,0,2:T(8,128)(2,1)}, u32[]{:S(2)}, u32[]{:S(2)}) async-start(bf16[2,64,32,128]{3,1,0,2:T(8,128)(2,1)} %copy_bitcast_fusion.1), calls=%async_computation.4 | async-start | bytes 2097152 | tf_op jit(solution)/shard_map/all_to_all | solution.py:92
  244.1 32.6 %all-to-all-start.5 = ((bf16[2,64,32,128]{3,1,0,2:T(8,128)(2,1)}), bf16[2,64,32,128]{3,1,0,2:T(8,128)(2,1)}, u32[]{:S(2)}, u32[]{:S(2)}) async-start(bf16[2,64,32,128]{3,1,0,2:T(8,128)(2,1)} %copy_bitcast_fusion), calls=%async_computation.5 | async-start | bytes 2097152 | tf_op jit(solution)/shard_map/all_to_all | solution.py:97
  248.9 4.7 %copy-start.10 = (bf16[2,64,32,128]{3,1,0,2:T(8,128)(2,1)S(1)}, bf16[2,64,32,128]{3,1,0,2:T(8,128)(2,1)}, u32[]{:S(2)}) copy-start(bf16[2,64,32,128]{3,1,0,2:T(8,128)(2,1)} %copy-done.9) | copy-start | bytes 3145732
  279.0 3.2 copy-start.4
  279.1 3.2 copy-start.6
  321.6 3.2 copy-start.2
  321.6 3.2 copy-start.7
  321.6 3.2 copy-start.4
  321.7 3.2 copy-start.6
  364.2 7.6 %copy-start.15 = (bf16[2,2048,128]{2,1,0:T(8,128)(2,1)S(1)}, bf16[2,2048,128]{2,1,0:T(8,128)(2,1)}, u32[]{:S(2)}) copy-start(bf16[2,2048,128]{2,1,0:T(8,128)(2,1)} %get-tuple-element.99) | copy-start | bytes 3145732
  367.9 31.9 %all-to-all-start.6 = ((bf16[2,2048,1,128]{3,0,2,1:T(2,128)(2,1)}), bf16[2,2048,1,128]{3,0,2,1:T(2,128)(2,1)S(1)}, u32[]{:S(2)}, u32[]{:S(2)}) async-start(bf16[2,2048,1,128]{3,0,2,1:T(2,128)(2,1)} %bitcast.124), calls=%async_computation.6 | async-start | bytes 2097152 | tf_op jit(solution)/shard_map/all_to_all | solution.py:102
  399.8 31.9 %all-to-all-start.7 = ((bf16[2,2048,1,128]{3,0,2,1:T(2,128)(2,1)}), bf16[2,2048,1,128]{3,0,2,1:T(2,128)(2,1)S(1)}, u32[]{:S(2)}, u32[]{:S(2)}) async-start(bf16[2,2048,1,128]{3,0,2,1:T(2,128)(2,1)} %bitcast.123), calls=%async_computation.7 | async-start | bytes 2097152 | tf_op jit(solution)/shard_map/all_to_all | solution.py:103
  (14 other events, 29.3 us)
where the time goes:
time: 435 us; the launch traced here: 434 us
  waiting for transfers between devices  167 us (38%)
  blocking collectives  86 us (20%)
  matrix products  66.8 us (15%)
  local copies, waits for them, and re-layouts  50.9 us (12%)
  starting transfers between devices  48.6 us (11%)
  other arithmetic  13.4 us (3%)
    all_gather x1, blocking collectives, on_device(): lax.all_gather(key_gain, 'dp', axis=0, tiled=True)  48 us
    all_gather x1, blocking collectives, on_device(): lax.all_gather(query_gain, 'dp', axis=0, tiled=True)  37.9 us
    all_to_all x1, waiting for transfers between devices, on_device(): lax.all_to_all(split(dkn), 'seq', split_axis=2, concat_axis=1, tiled=True)  26.7 us
    all_to_all x1, waiting for transfers between devices, on_device(): lax.all_to_all(split(qn), 'seq', split_axis=2, concat_axis=1, tiled=True)  26.6 us
    all_to_all x1, waiting for transfers between devices, on_device(): lax.all_to_all(split(value_rows), 'seq', split_axis=2, concat_axis=1, til...  25.5 us
    all_to_all x1, waiting for transfers between devices, on_device(): lax.all_to_all(split(kn), 'seq', split_axis=2, concat_axis=1, tiled=True)  25.4 us
    all_to_all x1, waiting for transfers between devices, on_device(): lax.all_to_all(attended_tangent, 'seq', split_axis=1, concat_axis=2, tile...  24 us
    all_to_all x1, waiting for transfers between devices, on_device(): lax.all_to_all(split(value_tangent), 'seq', split_axis=2, concat_axis=1,...  19.9 us
  transfers between devices with their start and end apart: 8, of which 7 were waited for; matrix products, arithmetic and copies ran while one was open for 8% of the time, Pallas kernels for 0%

commit v1 on v0

v1 whole, which is shorter than its diff:
```python
import jax
import jax.numpy as jnp
from jax import lax
from jax.experimental import pallas as pl
from jax.experimental.pallas import tpu as pltpu
from jax.sharding import PartitionSpec as P

EPS = 1e-06
DIM = 128
TILE = 256
MESH = pl.DeviceIdType.MESH
NT = (((1,), (1,)), ((), ()))
V, DV, K, DK, Q, DQ = range(6)


def attend(query, dquery, key, dkey, value, dvalue):
    scale = DIM**-0.5
    scores = lax.dot_general(query, key, NT, preferred_element_type=jnp.float32) * scale
    weights = jnp.exp(scores - jnp.max(scores, axis=-1, keepdims=True))
    weights = weights * (1.0 / jnp.sum(weights, axis=-1, keepdims=True))
    tangent = (
        lax.dot_general(
            jnp.concatenate([dquery, query], 1),
            jnp.concatenate([key, dkey], 1),
            NT,
            preferred_element_type=jnp.float32,
        )
        * scale
    )
    mean = jnp.sum(weights * tangent, axis=-1, keepdims=True)
    low = weights.astype(jnp.bfloat16)
    dlow = (weights * (tangent - mean)).astype(jnp.bfloat16)
    both = jnp.dot(low, jnp.concatenate([value, dvalue], 1), preferred_element_type=jnp.float32)
    dout = jnp.dot(dlow, value, preferred_element_type=jnp.float32) + both[:, DIM:]
    return both[:, :DIM].astype(jnp.bfloat16), dout.astype(jnp.bfloat16)


def make_kernel(seq, dp, clips, rows, width):
    per_tile = TILE // rows
    tiles = seq // per_tile

    def kernel(
        q_ref,
        k_ref,
        v_ref,
        dq_ref,
        dk_ref,
        dv_ref,
        gq_ref,
        gk_ref,
        o_ref,
        do_ref,
        normed,
        gathered,
        gains,
        held,
        results,
        load_sem,
        gain_send,
        gain_recv,
        send_sem,
        recv_sem,
        back_send,
        back_recv,
        own_sem,
        own_back,
    ):
        me = lax.axis_index("seq")
        group = lax.axis_index("dp")
        barrier = pltpu.get_barrier_semaphore()

        def greet_seq(r, carry):
            peer = lax.rem(me + r, seq)
            pl.semaphore_signal(barrier, inc=1, device_id={"seq": peer}, device_id_type=MESH)
            return carry

        def greet_dp(r, carry):
            peer = lax.rem(group + r, dp)
            pl.semaphore_signal(barrier, inc=1, device_id={"dp": peer}, device_id_type=MESH)
            return carry

        lax.fori_loop(1, dp, greet_dp, 0)
        lax.fori_loop(1, seq, greet_seq, 0)

        sources = {K: k_ref, DK: dk_ref, Q: q_ref, DQ: dq_ref}
        loads = [
            pltpu.make_async_copy(ref, normed.at[slot - K], load_sem.at[slot - K])
            for slot, ref in sources.items()
        ]
        gain_loads = [
            pltpu.make_async_copy(ref, gathered.at[which, group], load_sem.at[4 + which])
            for which, ref in enumerate((gq_ref, gk_ref))
        ]
        for copy in gain_loads + loads:
            copy.start()
        pl.semaphore_wait(barrier, seq + dp - 2)

        for which, ref in enumerate((gq_ref, gk_ref)):

            def send_gain(r, carry):
                peer = lax.rem(group + r, dp)
                pltpu.make_async_remote_copy(
                    src_ref=ref,
                    dst_ref=gathered.at[which, group],
                    send_sem=gain_send.at[which],
                    recv_sem=gain_recv.at[which],
                    device_id={"dp": peer},
                    device_id_type=MESH,
                ).start()
                return carry

            lax.fori_loop(1, dp, send_gain, 0)

        def source(clip, slot, head):
            columns = pl.ds(pl.multiple_of(head * DIM, DIM), DIM)
            if slot == V:
                return v_ref.at[clip, :, columns]
            if slot == DV:
                return dv_ref.at[clip, :, columns]
            return normed.at[slot - K, clip, :, columns]

        def send(clip, slot):
            def one(r, carry):
                head = lax.rem(me + r, seq)
                pltpu.make_async_remote_copy(
                    src_ref=source(clip, slot, head),
                    dst_ref=held.at[clip, slot, me],
                    send_sem=send_sem.at[clip, slot],
                    recv_sem=recv_sem.at[clip, slot],
                    device_id={"seq": head},
                    device_id_type=MESH,
                ).start()
                return carry

            lax.fori_loop(1, seq, one, 0)
            pltpu.make_async_copy(
                source(clip, slot, me), held.at[clip, slot, me], own_sem.at[clip, slot]
            ).start()

        def others(clip, slot):
            return held.at[clip, slot, pl.ds(0, seq - 1)]

        def arrive(clip, slot):
            pltpu.make_async_copy(
                others(clip, slot), others(clip, slot), recv_sem.at[clip, slot]
            ).wait()
            pltpu.make_async_copy(
                held.at[clip, slot, me], held.at[clip, slot, me], own_sem.at[clip, slot]
            ).wait()

        def normalize(clip, slot, which):
            def step(i, carry):
                part = pl.ds(pl.multiple_of(i * 16, 16), 16)
                x = normed[slot - K, clip, part, :].astype(jnp.float32)
                dx = normed[slot + 1 - K, clip, part, :].astype(jnp.float32)
                gain = gains[which]
                inverse = lax.rsqrt(jnp.sum(x * x, axis=-1, keepdims=True) * (1.0 / width) + EPS)
                cross = jnp.sum(x * dx, axis=-1, keepdims=True) * (1.0 / width)
                normed[slot - K, clip, part, :] = (x * inverse * gain).astype(jnp.bfloat16)
                normed[slot + 1 - K, clip, part, :] = (
                    (dx * inverse - x * (inverse * inverse * inverse * cross)) * gain
                ).astype(jnp.bfloat16)
                return carry

            lax.fori_loop(0, rows // 16, step, 0)

        send(0, V)
        send(0, DV)

        for which in range(2):
            gain_loads[which].wait()
            other = gathered.at[which, pl.ds(0, dp - 1)]
            pltpu.make_async_copy(other, other, gain_recv.at[which]).wait()
            chunks = width // dp // DIM
            for owner in range(dp):
                for j in range(chunks):
                    at = (owner * chunks + j) * DIM
                    gains[which, :, at : at + DIM] = gathered[which, owner, j : j + 1, :]
        for copy in loads:
            copy.wait()

        normalize(0, K, 1)
        send(0, K)
        send(0, DK)
        normalize(0, Q, 0)
        send(0, Q)
        send(0, DQ)
        for clip in range(1, clips):
            normalize(clip, K, 1)
            normalize(clip, Q, 0)

        chip_row, half = me // 8, (me % 8) // 4

        def tile_of(i):
            crosses = 1 - i // (tiles // 2)
            row = lax.rem(chip_row + i % (tiles // 2), tiles // 2)
            return row * 2 + (half + crosses) % 2

        def compute(clip, i):
            first = tile_of(i) * per_tile
            took = pl.ds(first, per_tile)

            def whole(slot):
                return held[clip, slot].reshape(seq * rows, DIM)

            out, dout = attend(
                held[clip, Q, took].reshape(TILE, DIM),
                held[clip, DQ, took].reshape(TILE, DIM),
                whole(K),
                whole(DK),
                whole(V),
                whole(DV),
            )
            results[clip, 0, took] = out.reshape(per_tile, rows, DIM)
            results[clip, 1, took] = dout.reshape(per_tile, rows, DIM)

        mine = pl.ds(pl.multiple_of(me * DIM, DIM), DIM)

        def give_back(clip, which, i):
            ref = (o_ref, do_ref)[which]
            first = tile_of(i) * per_tile
            for r in range(per_tile):
                token = first + r

                @pl.when(token != me)
                def _():
                    pltpu.make_async_remote_copy(
                        src_ref=results.at[clip, which, token],
                        dst_ref=ref.at[clip, :, mine],
                        send_sem=back_send.at[clip, which],
                        recv_sem=back_recv.at[clip, which],
                        device_id={"seq": token},
                        device_id_type=MESH,
                    ).start()

                @pl.when(token == me)
                def _():
                    pltpu.make_async_copy(
                        results.at[clip, which, token],
                        ref.at[clip, :, mine],
                        own_back.at[clip, which],
                    ).start()

        def loop(low, high, body):
            def step(i, carry):
                body(i)
                return carry

            lax.fori_loop(low, high, step, 0)

        send(1, V)
        arrive(0, V)
        send(1, DV)
        arrive(0, DV)
        send(1, K)
        arrive(0, K)
        arrive(0, DK)
        arrive(0, Q)
        arrive(0, DQ)
        send(1, DK)
        loop(0, 3, lambda i: compute(0, i))
        arrive(1, V)
        send(1, Q)
        loop(3, 6, lambda i: compute(0, i))
        arrive(1, DV)
        send(1, DQ)
        loop(6, tiles, lambda i: compute(0, i))
        arrive(1, K)
        arrive(1, DK)
        loop(0, tiles, lambda i: give_back(0, 0, i))
        arrive(1, Q)
        loop(0, tiles, lambda i: give_back(0, 1, i))
        arrive(1, DQ)

        def last(i):
            compute(1, i)
            give_back(1, 0, i)
            give_back(1, 1, i)

        loop(0, tiles, last)

        for which in range(2):
            other = gathered.at[which, pl.ds(0, dp - 1)]
            pltpu.make_async_copy(other, other, gain_send.at[which]).wait()
        for clip in range(clips):
            for slot in range(6):
                pltpu.make_async_copy(
                    others(clip, slot), others(clip, slot), send_sem.at[clip, slot]
                ).wait()
            for which in range(2):
                own, some = results.at[clip, which, 0], results.at[clip, which, pl.ds(0, seq - 1)]
                pltpu.make_async_copy(some, some, back_send.at[clip, which]).wait()
                pltpu.make_async_copy(own, own, own_back.at[clip, which]).wait()
                pltpu.make_async_copy(some, some, back_recv.at[clip, which]).wait()

    return kernel


def solution(mesh):
    seq, dp = mesh.shape["seq"], mesh.shape["dp"]

    def on_device(q, k, v, dq, dk, dv, gq, gk):
        clips, rows, width = q.shape
        gq, gk = (gain.reshape(gain.shape[0] // DIM, DIM) for gain in (gq, gk))
        out = jax.ShapeDtypeStruct(q.shape, q.dtype)
        pieces = clips * seq * seq * rows
        return pl.pallas_call(
            make_kernel(seq, dp, clips, rows, width),
            out_shape=(out, out),
            in_specs=[pl.BlockSpec(memory_space=pl.ANY)] * 8,
            out_specs=(pl.BlockSpec(memory_space=pl.ANY),) * 2,
            scratch_shapes=[
                pltpu.VMEM((4, clips, rows, width), jnp.bfloat16),
                pltpu.VMEM((2, dp) + gq.shape, jnp.float32),
                pltpu.VMEM((2, 1, width), jnp.float32),
                pltpu.VMEM((clips, 6, seq, rows, DIM), jnp.bfloat16),
                pltpu.VMEM((clips, 2, seq, rows, DIM), jnp.bfloat16),
                pltpu.SemaphoreType.DMA((6,)),
                pltpu.SemaphoreType.DMA((2,)),
                pltpu.SemaphoreType.DMA((2,)),
                pltpu.SemaphoreType.DMA((clips, 6)),
                pltpu.SemaphoreType.DMA((clips, 6)),
                pltpu.SemaphoreType.DMA((clips, 2)),
                pltpu.SemaphoreType.DMA((clips, 2)),
                pltpu.SemaphoreType.DMA((clips, 6)),
                pltpu.SemaphoreType.DMA((clips, 2)),
            ],
            compiler_params=pltpu.CompilerParams(
                collective_id=0, has_side_effects=True, vmem_limit_bytes=56 * 2**20
            ),
            cost_estimate=pl.CostEstimate(
                flops=12 * pieces * seq * rows * DIM // seq,
                bytes_accessed=8 * 2 * clips * rows * width,
                transcendentals=pieces * seq * rows // seq,
            ),
        )(q, k, v, dq, dk, dv, gq, gk)

    shard = P("dp", "seq", None)
    return jax.shard_map(
        on_device,
        mesh=mesh,
        in_specs=(shard,) * 6 + (P("dp"),) * 2,
        out_specs=(shard, shard),
        check_vma=False,
    )
```

time: 435 us -> 199 us (0.46)
  the two profiles are of different devices: /device:TPU:1 before, /device:TPU:37 now
where the time goes in v1:
time: 199 us; the launch traced here: 195 us
  Pallas kernels  191 us (96%)
  local copies, waits for them, and re-layouts  3.35 us (2%)
    pallas_call x1, Pallas kernels, on_device(): pl.pallas_call(make_kernel(seq, dp, clips, rows, width), out_shape=(out,...  191 us

profile of v1, /device:TPU:37, one launch (start us, length us, event | category | flops | bytes accessed | tf_op | source)
XLA Modules:
  0.0 195.2 jit_solution(5549290370577988732)
XLA Ops:
  0.6 191.2 %shard_map.95 = (bf16[2,64,4096]{2,1,0:T(8,128)(2,1)}, bf16[2,64,4096]{2,1,0:T(8,128)(2,1)}) custom-call(bf16[2,64,4096]{2,1,0:T(8,128)(2,1)} %q_ref.1, bf16[2,64,4096]{2,1,0:T(8,128)(2,1)} %k_ref.1, bf16[2,64,4096]{2,1,0:T(8,128)(2,1)} %v_ref.1, bf16[2,64,4096]{2,1,0:T(8,128)(2,1)} %dq_ref.1, bf16[2,64,4096]{2,1,0:T(8,128)(2,1)} %dk_ref.1, ...), custom_call_target="tpu_custom_call" | custom-call | flops 12884901888 | bytes 8388608 | tf_op jit(solution)/shard_map/pallas_call | solution.py:307
  191.8 0.0 copy-start
  191.8 2.4 %copy.12 = bf16[2,64,4096]{2,1,0:T(8,128)(2,1)} copy(bf16[2,64,4096]{2,1,0:T(8,128)(2,1)} %get-tuple-element.4) | data formatting | bytes 2097152
  194.2 0.0 copy-done
  194.2 1.0 copy.13
Async XLA Ops:
  191.8 2.4 %copy-start = (bf16[2,64,4096]{2,1,0:T(8,128)(2,1)S(1)}, bf16[2,64,4096]{2,1,0:T(8,128)(2,1)}, u32[]{:S(2)}) copy-start(bf16[2,64,4096]{2,1,0:T(8,128)(2,1)} %get-tuple-element.5) | copy-start | bytes 3145732

commit v2 on v1

--- a/solution.py
+++ b/solution.py
@@ -35,8 +35,20 @@
     return both[:, :DIM].astype(jnp.bfloat16), dout.astype(jnp.bfloat16)
 
 
+def write_out(a_ref, b_ref, o_ref, do_ref, sem):
+    copies = [
+        pltpu.make_async_copy(a_ref, o_ref, sem.at[0]),
+        pltpu.make_async_copy(b_ref, do_ref, sem.at[1]),
+    ]
+    for copy in copies:
+        copy.start()
+    for copy in copies:
+        copy.wait()
+
+
 def make_kernel(seq, dp, clips, rows, width):
     per_tile = TILE // rows
+    plane = 8
     tiles = seq // per_tile
 
     def kernel(
@@ -58,6 +70,9 @@
         load_sem,
         gain_send,
         gain_recv,
+        hand_send,
+        hand_recv,
+        entered,
         send_sem,
         recv_sem,
         back_send,
@@ -67,11 +82,17 @@
     ):
         me = lax.axis_index("seq")
         group = lax.axis_index("dp")
+        gate = jnp.logical_and(me // plane == 0, me % 2 == 0)
+        beside = jnp.logical_and(me // plane == 0, me % 2 == 1)
         barrier = pltpu.get_barrier_semaphore()
 
         def greet_seq(r, carry):
             peer = lax.rem(me + r, seq)
-            pl.semaphore_signal(barrier, inc=1, device_id={"seq": peer}, device_id_type=MESH)
+
+            @pl.when(jnp.logical_or(peer // plane > 0, peer % 2 == 1))
+            def _():
+                pl.semaphore_signal(barrier, inc=1, device_id={"seq": peer}, device_id_type=MESH)
+
             return carry
 
         def greet_dp(r, carry):
@@ -79,37 +100,73 @@
             pl.semaphore_signal(barrier, inc=1, device_id={"dp": peer}, device_id_type=MESH)
             return carry
 
-        lax.fori_loop(1, dp, greet_dp, 0)
         lax.fori_loop(1, seq, greet_seq, 0)
+
+        @pl.when(gate)
+        def _():
+            lax.fori_loop(1, dp, greet_dp, 0)
 
         sources = {K: k_ref, DK: dk_ref, Q: q_ref, DQ: dq_ref}
         loads = [
             pltpu.make_async_copy(ref, normed.at[slot - K], load_sem.at[slot - K])
             for slot, ref in sources.items()
         ]
-        gain_loads = [
-            pltpu.make_async_copy(ref, gathered.at[which, group], load_sem.at[4 + which])
-            for which, ref in enumerate((gq_ref, gk_ref))
-        ]
-        for copy in gain_loads + loads:
+        for copy in loads:
             copy.start()
-        pl.semaphore_wait(barrier, seq + dp - 2)
-
-        for which, ref in enumerate((gq_ref, gk_ref)):
-
-            def send_gain(r, carry):
-                peer = lax.rem(group + r, dp)
+
+        @pl.when(jnp.logical_not(gate))
+        def _():
+            pl.semaphore_wait(barrier, seq - 1)
+
+        @pl.when(beside)
+        def _():
+            pl.semaphore_signal(entered, inc=1, device_id={"seq": me - 1}, device_id_type=MESH)
+
+        @pl.when(gate)
+        def _():
+            pl.semaphore_wait(entered, 1)
+
+        def exchange_gains():
+            gain_loads = [
+                pltpu.make_async_copy(ref, gathered.at[which, group], load_sem.at[4 + which])
+                for which, ref in enumerate((gq_ref, gk_ref))
+            ]
+            for copy in gain_loads:
+                copy.start()
+            pl.semaphore_wait(barrier, dp - 1)
+            for which, ref in enumerate((gq_ref, gk_ref)):
+
+                def send_gain(r, carry):
+                    peer = lax.rem(group + r, dp)
+                    pltpu.make_async_remote_copy(
+                        src_ref=ref,
+                        dst_ref=gathered.at[which, group],
+                        send_sem=gain_send.at[which],
+                        recv_sem=gain_recv.at[which],
+                        device_id={"dp": peer},
+                        device_id_type=MESH,
+                    ).start()
+                    return carry
+
+                lax.fori_loop(1, dp, send_gain, 0)
+            for which in range(2):
+                gain_loads[which].wait()
+                other = gathered.at[which, pl.ds(0, dp - 1)]
+                pltpu.make_async_copy(other, other, gain_recv.at[which]).wait()
+
+            def hand_on(r, carry):
+                peer = me + lax.rem(r, 2) + r // 2 * plane
                 pltpu.make_async_remote_copy(
-                    src_ref=ref,
-                    dst_ref=gathered.at[which, group],
-                    send_sem=gain_send.at[which],
-                    recv_sem=gain_recv.at[which],
-                    device_id={"dp": peer},
+                    src_ref=gathered,
+                    dst_ref=gathered,
+                    send_sem=hand_send.at[r],
+                    recv_sem=hand_recv,
+                    device_id={"seq": peer},
                     device_id_type=MESH,
                 ).start()
                 return carry
 
-            lax.fori_loop(1, dp, send_gain, 0)
+            lax.fori_loop(1, seq // plane * 2, hand_on, 0)
 
         def source(clip, slot, head):
             columns = pl.ds(pl.multiple_of(head * DIM, DIM), DIM)
@@ -167,10 +224,13 @@
         send(0, V)
         send(0, DV)
 
+        pl.when(gate)(exchange_gains)
+
+        @pl.when(jnp.logical_not(gate))
+        def _():
+            pltpu.make_async_copy(gathered, gathered, hand_recv).wait()
+
         for which in range(2):
-            gain_loads[which].wait()
-            other = gathered.at[which, pl.ds(0, dp - 1)]
-            pltpu.make_async_copy(other, other, gain_recv.at[which]).wait()
             chunks = width // dp // DIM
             for owner in range(dp):
                 for j in range(chunks):
@@ -189,11 +249,11 @@
             normalize(clip, K, 1)
             normalize(clip, Q, 0)
 
-        chip_row, half = me // 8, (me % 8) // 4
+        chip_row, half = me // plane, me % plane // 4
 
         def tile_of(i):
-            crosses = 1 - i // (tiles // 2)
-            row = lax.rem(chip_row + i % (tiles // 2), tiles // 2)
+            crosses = i % 2
+            row = lax.rem(chip_row + i // 2, tiles // 2)
             return row * 2 + (half + crosses) % 2
 
         def compute(clip, i):
@@ -279,9 +339,18 @@
 
         loop(0, tiles, last)
 
-        for which in range(2):
-            other = gathered.at[which, pl.ds(0, dp - 1)]
-            pltpu.make_async_copy(other, other, gain_send.at[which]).wait()
+        @pl.when(gate)
+        def _():
+            for which in range(2):
+                other = gathered.at[which, pl.ds(0, dp - 1)]
+                pltpu.make_async_copy(other, other, gain_send.at[which]).wait()
+
+            def handed(r, carry):
+                pltpu.make_async_copy(gathered, gathered, hand_send.at[r]).wait()
+                return carry
+
+            lax.fori_loop(1, seq // plane * 2, handed, 0)
+
         for clip in range(clips):
             for slot in range(6):
                 pltpu.make_async_copy(
@@ -302,13 +371,12 @@
     def on_device(q, k, v, dq, dk, dv, gq, gk):
         clips, rows, width = q.shape
         gq, gk = (gain.reshape(gain.shape[0] // DIM, DIM) for gain in (gq, gk))
-        out = jax.ShapeDtypeStruct(q.shape, q.dtype)
         pieces = clips * seq * seq * rows
-        return pl.pallas_call(
+        rows_out = pl.pallas_call(
             make_kernel(seq, dp, clips, rows, width),
-            out_shape=(out, out),
+            out_shape=(pltpu.VMEM(q.shape, q.dtype),) * 2,
             in_specs=[pl.BlockSpec(memory_space=pl.ANY)] * 8,
-            out_specs=(pl.BlockSpec(memory_space=pl.ANY),) * 2,
+            out_specs=(pl.BlockSpec(memory_space=pltpu.VMEM),) * 2,
             scratch_shapes=[
                 pltpu.VMEM((4, clips, rows, width), jnp.bfloat16),
                 pltpu.VMEM((2, dp) + gq.shape, jnp.float32),
@@ -318,6 +386,9 @@
                 pltpu.SemaphoreType.DMA((6,)),
                 pltpu.SemaphoreType.DMA((2,)),
                 pltpu.SemaphoreType.DMA((2,)),
+                pltpu.SemaphoreType.DMA((8,)),
+                pltpu.SemaphoreType.DMA,
+                pltpu.SemaphoreType.REGULAR,
                 pltpu.SemaphoreType.DMA((clips, 6)),
                 pltpu.SemaphoreType.DMA((clips, 6)),
                 pltpu.SemaphoreType.DMA((clips, 2)),
@@ -326,14 +397,22 @@
                 pltpu.SemaphoreType.DMA((clips, 2)),
             ],
             compiler_params=pltpu.CompilerParams(
-                collective_id=0, has_side_effects=True, vmem_limit_bytes=56 * 2**20
+                collective_id=0, has_side_effects=True, vmem_limit_bytes=48 * 2**20
             ),
             cost_estimate=pl.CostEstimate(
                 flops=12 * pieces * seq * rows * DIM // seq,
                 bytes_accessed=8 * 2 * clips * rows * width,
                 transcendentals=pieces * seq * rows // seq,
             ),
-        )(q, k, v, dq, dk, dv, gq, gk)
+        )(*(pltpu.with_memory_space_constraint(x, pltpu.HBM) for x in (q, k, v, dq, dk, dv, gq, gk)))
+        out = jax.ShapeDtypeStruct(q.shape, q.dtype)
+        return pl.pallas_call(
+            write_out,
+            out_shape=(out, out),
+            in_specs=[pl.BlockSpec(memory_space=pltpu.VMEM)] * 2,
+            out_specs=(pl.BlockSpec(memory_space=pl.ANY),) * 2,
+            scratch_shapes=[pltpu.SemaphoreType.DMA((2,))],
+        )(*(pltpu.with_memory_space_constraint(x, pltpu.VMEM) for x in rows_out))
 
     shard = P("dp", "seq", None)
     return jax.shard_map(

time: 199 us -> 194 us (0.975)
  local copies, waits for them, and re-layouts: 3.35 us -> 0 us
    unnamed x4 -> x0, local copies, waits for them, and re-layouts: 3.35 us -> none
    pallas_call x1 -> x2, Pallas kernels: 191 us -> 191 us  [the longest x1 190 us: on_device(): pl.pallas_call(make_kernel(seq, dp, clips, rows, width), out_shape=(pltpu...]
where the time goes in v2:
time: 194 us; the launch traced here: 192 us
  Pallas kernels  191 us (98%)
    pallas_call x1, Pallas kernels, on_device(): pl.pallas_call(make_kernel(seq, dp, clips, rows, width), out_shape=(pltpu...  190 us

profile of v2, /device:TPU:37, one launch (start us, length us, event | category | flops | bytes accessed | tf_op | source)
XLA Modules:
  0.0 192.1 jit_solution(2326806000705691119)
XLA Ops:
  0.6 190.1 %shard_map.95 = (bf16[2,64,4096]{2,1,0:T(8,128)(2,1)S(1)}, bf16[2,64,4096]{2,1,0:T(8,128)(2,1)S(1)}) custom-call(bf16[2,64,4096]{2,1,0:T(8,128)(2,1)} %q_ref.1, bf16[2,64,4096]{2,1,0:T(8,128)(2,1)} %k_ref.1, bf16[2,64,4096]{2,1,0:T(8,128)(2,1)} %v_ref.1, bf16[2,64,4096]{2,1,0:T(8,128)(2,1)} %dq_ref.1, bf16[2,64,4096]{2,1,0:T(8,128)(2,1)} %dk_ref.1, ...), custom_call_target="tpu_custom_call" | custom-call | flops 12884901888 | bytes 8388608 | tf_op jit(solution)/shard_map/pallas_call | solution.py:375
  190.7 1.3 shard_map.96

commit v3 on v2

--- a/solution.py
+++ b/solution.py
@@ -82,14 +82,14 @@
     ):
         me = lax.axis_index("seq")
         group = lax.axis_index("dp")
-        gate = jnp.logical_and(me // plane == 0, me % 2 == 0)
-        beside = jnp.logical_and(me // plane == 0, me % 2 == 1)
+        gate = me % (plane + 2) == 0
+        beside = me % (plane + 2) == 1
         barrier = pltpu.get_barrier_semaphore()
 
         def greet_seq(r, carry):
-            peer = lax.rem(me + r, seq)
-
-            @pl.when(jnp.logical_or(peer // plane > 0, peer % 2 == 1))
+            peer = lax.rem(me - r + seq, seq)
+
+            @pl.when(peer % (plane + 2) != 0)
             def _():
                 pl.semaphore_signal(barrier, inc=1, device_id={"seq": peer}, device_id_type=MESH)
 
@@ -126,11 +126,12 @@
         def _():
             pl.semaphore_wait(entered, 1)
 
-        def exchange_gains():
-            gain_loads = [
-                pltpu.make_async_copy(ref, gathered.at[which, group], load_sem.at[4 + which])
-                for which, ref in enumerate((gq_ref, gk_ref))
-            ]
+        gain_loads = [
+            pltpu.make_async_copy(ref, gathered.at[which, group], load_sem.at[4 + which])
+            for which, ref in enumerate((gq_ref, gk_ref))
+        ]
+
+        def send_gains():
             for copy in gain_loads:
                 copy.start()
             pl.semaphore_wait(barrier, dp - 1)
@@ -149,13 +150,15 @@
                     return carry
 
                 lax.fori_loop(1, dp, send_gain, 0)
+
+        def hand_gains():
             for which in range(2):
                 gain_loads[which].wait()
                 other = gathered.at[which, pl.ds(0, dp - 1)]
                 pltpu.make_async_copy(other, other, gain_recv.at[which]).wait()
 
             def hand_on(r, carry):
-                peer = me + lax.rem(r, 2) + r // 2 * plane
+                peer = lax.rem(me + lax.rem(r, 2) + r // 2 * plane, seq)
                 pltpu.make_async_remote_copy(
                     src_ref=gathered,
                     dst_ref=gathered,
@@ -222,9 +225,12 @@
             lax.fori_loop(0, rows // 16, step, 0)
 
         send(0, V)
+        pl.when(gate)(send_gains)
         send(0, DV)
-
-        pl.when(gate)(exchange_gains)
+        pl.when(gate)(hand_gains)
+        for clip in range(1, clips):
+            send(clip, V)
+            send(clip, DV)
 
         @pl.when(jnp.logical_not(gate))
         def _():
@@ -243,8 +249,6 @@
         send(0, K)
         send(0, DK)
         normalize(0, Q, 0)
-        send(0, Q)
-        send(0, DQ)
         for clip in range(1, clips):
             normalize(clip, K, 1)
             normalize(clip, Q, 0)
@@ -253,7 +257,7 @@
 
         def tile_of(i):
             crosses = i % 2
-            row = lax.rem(chip_row + i // 2, tiles // 2)
+            row = lax.rem(chip_row + i // 2 + 1, tiles // 2)
             return row * 2 + (half + crosses) % 2
 
         def compute(clip, i):
@@ -280,7 +284,7 @@
             ref = (o_ref, do_ref)[which]
             first = tile_of(i) * per_tile
             for r in range(per_tile):
-                token = first + r
+                token = first + half * r + (1 - half) * (per_tile - 1 - r)
 
                 @pl.when(token != me)
                 def _():
@@ -308,29 +312,27 @@
 
             lax.fori_loop(low, high, step, 0)
 
-        send(1, V)
         arrive(0, V)
-        send(1, DV)
+        send(0, Q)
         arrive(0, DV)
+        send(0, DQ)
+        arrive(1, V)
         send(1, K)
+        arrive(1, DV)
+        send(1, DK)
         arrive(0, K)
+        send(1, Q)
         arrive(0, DK)
+        send(1, DQ)
         arrive(0, Q)
         arrive(0, DQ)
-        send(1, DK)
-        loop(0, 3, lambda i: compute(0, i))
-        arrive(1, V)
-        send(1, Q)
-        loop(3, 6, lambda i: compute(0, i))
-        arrive(1, DV)
-        send(1, DQ)
-        loop(6, tiles, lambda i: compute(0, i))
+        loop(0, tiles, lambda i: compute(0, i))
         arrive(1, K)
         arrive(1, DK)
         loop(0, tiles, lambda i: give_back(0, 0, i))
         arrive(1, Q)
+        arrive(1, DQ)
         loop(0, tiles, lambda i: give_back(0, 1, i))
-        arrive(1, DQ)
 
         def last(i):
             compute(1, i)

time: 194 us -> 192 us (0.990)
  no operation moved by 1% of the time
where the time goes in v3:
time: 192 us; the launch traced here: 191 us
  Pallas kernels  190 us (99%)
    pallas_call x1, Pallas kernels, on_device(): pl.pallas_call(make_kernel(seq, dp, clips, rows, width), out_shape=(pltpu...  189 us

profile of v3, /device:TPU:37, one launch (start us, length us, event | category | flops | bytes accessed | tf_op | source)
XLA Modules:
  0.0 190.6 jit_solution(9534363191860051755)
XLA Ops:
  0.6 188.6 %shard_map.95 = (bf16[2,64,4096]{2,1,0:T(8,128)(2,1)S(1)}, bf16[2,64,4096]{2,1,0:T(8,128)(2,1)S(1)}) custom-call(bf16[2,64,4096]{2,1,0:T(8,128)(2,1)} %q_ref.1, bf16[2,64,4096]{2,1,0:T(8,128)(2,1)} %k_ref.1, bf16[2,64,4096]{2,1,0:T(8,128)(2,1)} %v_ref.1, bf16[2,64,4096]{2,1,0:T(8,128)(2,1)} %dq_ref.1, bf16[2,64,4096]{2,1,0:T(8,128)(2,1)} %dk_ref.1, ...), custom_call_target="tpu_custom_call" | custom-call | flops 12884901888 | bytes 8388608 | tf_op jit(solution)/shard_map/pallas_call | solution.py:377
  189.2 1.3 shard_map.96

commit v4 on v3

--- a/solution.py
+++ b/solution.py
@@ -82,17 +82,24 @@
     ):
         me = lax.axis_index("seq")
         group = lax.axis_index("dp")
-        gate = me % (plane + 2) == 0
-        beside = me % (plane + 2) == 1
+        row, z, core = me // plane, me % plane // 2, me % 2
+        half = z // 2
+        gate = me % (plane + 2) == 1
+        listener = jnp.logical_and(core == 1, jnp.logical_not(gate))
+        across = 2 - half
         barrier = pltpu.get_barrier_semaphore()
 
-        def greet_seq(r, carry):
+        def greet(peer):
+            pl.semaphore_signal(barrier, inc=1, device_id={"seq": peer}, device_id_type=MESH)
+
+        @pl.when(jnp.logical_or(z == 1, z == 2))
+        def _():
+            for k in range(2):
+                greet(row * plane + (2 * (2 - z) + k) * 2)
+
+        def greet_listener(r, carry):
             peer = lax.rem(me - r + seq, seq)
-
-            @pl.when(peer % (plane + 2) != 0)
-            def _():
-                pl.semaphore_signal(barrier, inc=1, device_id={"seq": peer}, device_id_type=MESH)
-
+            pl.when(jnp.logical_and(peer % 2 == 1, peer % (plane + 2) != 1))(lambda: greet(peer))
             return carry
 
         def greet_dp(r, carry):
@@ -100,11 +107,40 @@
             pl.semaphore_signal(barrier, inc=1, device_id={"dp": peer}, device_id_type=MESH)
             return carry
 
-        lax.fori_loop(1, seq, greet_seq, 0)
+        lax.fori_loop(1, seq, greet_listener, 0)
 
         @pl.when(gate)
         def _():
             lax.fori_loop(1, dp, greet_dp, 0)
+
+        def source(clip, slot, head):
+            columns = pl.ds(pl.multiple_of(head * DIM, DIM), DIM)
+            if slot == V:
+                return v_ref.at[clip, :, columns]
+            if slot == DV:
+                return dv_ref.at[clip, :, columns]
+            return normed.at[slot - K, clip, :, columns]
+
+        def send_one(clip, slot, head):
+            pltpu.make_async_remote_copy(
+                src_ref=source(clip, slot, head),
+                dst_ref=held.at[clip, slot, me],
+                send_sem=send_sem.at[clip, slot],
+                recv_sem=recv_sem.at[clip, slot],
+                device_id={"seq": head},
+                device_id_type=MESH,
+            ).start()
+
+        def send_early():
+            for clip in range(clips):
+                for slot in (V, DV):
+                    for k in range(2):
+                        send_one(clip, slot, row * plane + across * 2 + k)
+
+        @pl.when(core == 0)
+        def _():
+            pl.semaphore_wait(barrier, 2)
+            send_early()
 
         sources = {K: k_ref, DK: dk_ref, Q: q_ref, DQ: dq_ref}
         loads = [
@@ -114,15 +150,20 @@
         for copy in loads:
             copy.start()
 
-        @pl.when(jnp.logical_not(gate))
+        def admit(peer):
+            pl.semaphore_signal(entered, inc=1, device_id={"seq": peer}, device_id_type=MESH)
+
+        @pl.when(listener)
         def _():
             pl.semaphore_wait(barrier, seq - 1)
-
-        @pl.when(beside)
-        def _():
-            pl.semaphore_signal(entered, inc=1, device_id={"seq": me - 1}, device_id_type=MESH)
-
-        @pl.when(gate)
+            admit(me - 1)
+
+            @pl.when(row == lax.rem(z + 1, seq // plane))
+            def _():
+                admit(z * (plane + 2))
+                admit(z * (plane + 2) + 1)
+
+        @pl.when(jnp.logical_not(listener))
         def _():
             pl.semaphore_wait(entered, 1)
 
@@ -158,7 +199,8 @@
                 pltpu.make_async_copy(other, other, gain_recv.at[which]).wait()
 
             def hand_on(r, carry):
-                peer = lax.rem(me + lax.rem(r, 2) + r // 2 * plane, seq)
+                step = lax.rem(r + 1, plane)
+                peer = lax.rem(me - 1 + step % 2 + step // 2 * plane, seq)
                 pltpu.make_async_remote_copy(
                     src_ref=gathered,
                     dst_ref=gathered,
@@ -171,25 +213,14 @@
 
             lax.fori_loop(1, seq // plane * 2, hand_on, 0)
 
-        def source(clip, slot, head):
-            columns = pl.ds(pl.multiple_of(head * DIM, DIM), DIM)
-            if slot == V:
-                return v_ref.at[clip, :, columns]
-            if slot == DV:
-                return dv_ref.at[clip, :, columns]
-            return normed.at[slot - K, clip, :, columns]
-
         def send(clip, slot):
             def one(r, carry):
                 head = lax.rem(me + r, seq)
-                pltpu.make_async_remote_copy(
-                    src_ref=source(clip, slot, head),
-                    dst_ref=held.at[clip, slot, me],
-                    send_sem=send_sem.at[clip, slot],
-                    recv_sem=recv_sem.at[clip, slot],
-                    device_id={"seq": head},
-                    device_id_type=MESH,
-                ).start()
+                if slot in (V, DV):
+                    sent = jnp.logical_and(core == 0, head // 2 == row * (plane // 2) + across)
+                    pl.when(jnp.logical_not(sent))(lambda: send_one(clip, slot, head))
+                else:
+                    send_one(clip, slot, head)
                 return carry
 
             lax.fori_loop(1, seq, one, 0)
@@ -253,12 +284,9 @@
             normalize(clip, K, 1)
             normalize(clip, Q, 0)
 
-        chip_row, half = me // plane, me % plane // 4
-
         def tile_of(i):
             crosses = i % 2
-            row = lax.rem(chip_row + i // 2 + 1, tiles // 2)
-            return row * 2 + (half + crosses) % 2
+            return lax.rem(row + i // 2 + 1, tiles // 2) * 2 + (half + crosses) % 2
 
         def compute(clip, i):
             first = tile_of(i) * per_tile

time: 192 us -> 190 us (0.990)
  Pallas kernels: 190 us -> 187 us
    pallas_call x1, Pallas kernels: 189 us -> 186 us  [on_device(): pl.pallas_call(make_kernel(seq, dp, clips, rows, width), out_shape=(pltpu...]
where the time goes in v4:
time: 190 us; the launch traced here: 188 us
  Pallas kernels  187 us (98%)
    pallas_call x1, Pallas kernels, on_device(): pl.pallas_call(make_kernel(seq, dp, clips, rows, width), out_shape=(pltpu...  186 us

profile of v4, /device:TPU:37, one launch (start us, length us, event | category | flops | bytes accessed | tf_op | source)
XLA Modules:
  0.0 187.8 jit_solution(180510616574633289)
XLA Ops:
  0.6 185.9 %shard_map.95 = (bf16[2,64,4096]{2,1,0:T(8,128)(2,1)S(1)}, bf16[2,64,4096]{2,1,0:T(8,128)(2,1)S(1)}) custom-call(bf16[2,64,4096]{2,1,0:T(8,128)(2,1)} %q_ref.1, bf16[2,64,4096]{2,1,0:T(8,128)(2,1)} %k_ref.1, bf16[2,64,4096]{2,1,0:T(8,128)(2,1)} %v_ref.1, bf16[2,64,4096]{2,1,0:T(8,128)(2,1)} %dq_ref.1, bf16[2,64,4096]{2,1,0:T(8,128)(2,1)} %dk_ref.1, ...), custom_call_target="tpu_custom_call" | custom-call | flops 12884901888 | bytes 8388608 | tf_op jit(solution)/shard_map/pallas_call | solution.py:405
  186.5 1.3 shard_map.96

commit v5 on v4

--- a/solution.py
+++ b/solution.py
@@ -86,16 +86,15 @@
         half = z // 2
         gate = me % (plane + 2) == 1
         listener = jnp.logical_and(core == 1, jnp.logical_not(gate))
-        across = 2 - half
         barrier = pltpu.get_barrier_semaphore()
 
         def greet(peer):
             pl.semaphore_signal(barrier, inc=1, device_id={"seq": peer}, device_id_type=MESH)
 
-        @pl.when(jnp.logical_or(z == 1, z == 2))
+        @pl.when(z < 3)
         def _():
             for k in range(2):
-                greet(row * plane + (2 * (2 - z) + k) * 2)
+                greet(row * plane + (2 * (1 - half) + k) * 2)
 
         def greet_listener(r, carry):
             peer = lax.rem(me - r + seq, seq)
@@ -131,16 +130,22 @@
                 device_id_type=MESH,
             ).start()
 
-        def send_early():
+        def send_early(to):
             for clip in range(clips):
                 for slot in (V, DV):
                     for k in range(2):
-                        send_one(clip, slot, row * plane + across * 2 + k)
-
-        @pl.when(core == 0)
+                        send_one(clip, slot, row * plane + to * 2 + k)
+
+        @pl.when(jnp.logical_and(core == 0, half == 0))
         def _():
             pl.semaphore_wait(barrier, 2)
-            send_early()
+            send_early(2)
+
+        @pl.when(jnp.logical_and(core == 0, half == 1))
+        def _():
+            pl.semaphore_wait(barrier, 4)
+            send_early(0)
+            send_early(1)
 
         sources = {K: k_ref, DK: dk_ref, Q: q_ref, DQ: dq_ref}
         loads = [
@@ -217,7 +222,9 @@
             def one(r, carry):
                 head = lax.rem(me + r, seq)
                 if slot in (V, DV):
-                    sent = jnp.logical_and(core == 0, head // 2 == row * (plane // 2) + across)
+                    to = head % plane // 2
+                    told = jnp.logical_or(to == 2 - 2 * half, to == 2 - half)
+                    sent = jnp.logical_and(core == 0, jnp.logical_and(head // plane == row, told))
                     pl.when(jnp.logical_not(sent))(lambda: send_one(clip, slot, head))
                 else:
                     send_one(clip, slot, head)
@@ -308,10 +315,10 @@
 
         mine = pl.ds(pl.multiple_of(me * DIM, DIM), DIM)
 
-        def give_back(clip, which, i):
+        def give_back(clip, which, i, pieces=range(per_tile)):
             ref = (o_ref, do_ref)[which]
             first = tile_of(i) * per_tile
-            for r in range(per_tile):
+            for r in pieces:
                 token = first + half * r + (1 - half) * (per_tile - 1 - r)
 
                 @pl.when(token != me)
@@ -364,10 +371,23 @@
 
         def last(i):
             compute(1, i)
-            give_back(1, 0, i)
-            give_back(1, 1, i)
+            for which in range(2):
+                give_back(1, which, i, range(per_tile // 2))
+
+            @pl.when(jnp.logical_or(half == 0, i % 2 == 0))
+            def _():
+                for which in range(2):
+                    give_back(1, which, i, range(per_tile // 2, per_tile))
 
         loop(0, tiles, last)
+
+        @pl.when(half == 1)
+        def _():
+            def rest(i):
+                for which in range(2):
+                    give_back(1, which, 2 * i + 1, range(per_tile // 2, per_tile))
+
+            loop(0, tiles // 2, rest)
 
         @pl.when(gate)
         def _():

time: 190 us -> 189 us (level)
  no operation moved by 1% of the time
where the time goes in v5:
time: 189 us; the launch traced here: 188 us
  Pallas kernels  188 us (99%)
    pallas_call x1, Pallas kernels, on_device(): pl.pallas_call(make_kernel(seq, dp, clips, rows, width), out_shape=(pltpu...  187 us

profile of v5, /device:TPU:37, one launch (start us, length us, event | category | flops | bytes accessed | tf_op | source)
XLA Modules:
  0.0 188.5 jit_solution(8916297464428035909)
XLA Ops:
  0.6 186.5 %shard_map.95 = (bf16[2,64,4096]{2,1,0:T(8,128)(2,1)S(1)}, bf16[2,64,4096]{2,1,0:T(8,128)(2,1)S(1)}) custom-call(bf16[2,64,4096]{2,1,0:T(8,128)(2,1)} %q_ref.1, bf16[2,64,4096]{2,1,0:T(8,128)(2,1)} %k_ref.1, bf16[2,64,4096]{2,1,0:T(8,128)(2,1)} %v_ref.1, bf16[2,64,4096]{2,1,0:T(8,128)(2,1)} %dq_ref.1, bf16[2,64,4096]{2,1,0:T(8,128)(2,1)} %dk_ref.1, ...), custom_call_target="tpu_custom_call" | custom-call | flops 12884901888 | bytes 8388608 | tf_op jit(solution)/shard_map/pallas_call | solution.py:425
  187.2 1.3 shard_map.96

commit v6 on v5

--- a/solution.py
+++ b/solution.py
@@ -1,3 +1,5 @@
+import functools
+
 import jax
 import jax.numpy as jnp
 from jax import lax
@@ -82,31 +84,43 @@
     ):
         me = lax.axis_index("seq")
         group = lax.axis_index("dp")
-        row, z, core = me // plane, me % plane // 2, me % 2
+        row, z = me // plane, me % plane // 2
         half = z // 2
-        gate = me % (plane + 2) == 1
-        listener = jnp.logical_and(core == 1, jnp.logical_not(gate))
+
+        gates, listeners = ((at * plane + 3, at * plane + 5) for at in (2, 3))
+
+        def is_gate(device):
+            return jnp.logical_or(device == gates[0], device == gates[1])
+
+        def is_listener(device):
+            return jnp.logical_or(device == listeners[0], device == listeners[1])
+
+        def is_common(device):
+            return jnp.logical_not(jnp.logical_or(is_gate(device), is_listener(device)))
+
+        def in_half(r):
+            at = lax.rem(row * 4 + me % 4 + r, seq // 2)
+            return at // 4 * plane + half * 4 + at % 4
+
+        gate, listener, common = is_gate(me), is_listener(me), is_common(me)
         barrier = pltpu.get_barrier_semaphore()
 
         def greet(peer):
             pl.semaphore_signal(barrier, inc=1, device_id={"seq": peer}, device_id_type=MESH)
 
+        for peer in listeners:
+            pl.when(me != peer)(functools.partial(greet, peer))
+
         @pl.when(z < 3)
         def _():
-            for k in range(2):
-                greet(row * plane + (2 * (1 - half) + k) * 2)
-
-        def greet_listener(r, carry):
-            peer = lax.rem(me - r + seq, seq)
-            pl.when(jnp.logical_and(peer % 2 == 1, peer % (plane + 2) != 1))(lambda: greet(peer))
-            return carry
+            for k in range(4):
+                peer = row * plane + (1 - half) * 4 + k
+                pl.when(is_common(peer))(functools.partial(greet, peer))
 
         def greet_dp(r, carry):
             peer = lax.rem(group + r, dp)
             pl.semaphore_signal(barrier, inc=1, device_id={"dp": peer}, device_id_type=MESH)
             return carry
-
-        lax.fori_loop(1, seq, greet_listener, 0)
 
         @pl.when(gate)
         def _():
@@ -136,12 +150,12 @@
                     for k in range(2):
                         send_one(clip, slot, row * plane + to * 2 + k)
 
-        @pl.when(jnp.logical_and(core == 0, half == 0))
+        @pl.when(jnp.logical_and(common, half == 0))
         def _():
             pl.semaphore_wait(barrier, 2)
             send_early(2)
 
-        @pl.when(jnp.logical_and(core == 0, half == 1))
+        @pl.when(jnp.logical_and(common, half == 1))
         def _():
             pl.semaphore_wait(barrier, 4)
             send_early(0)
@@ -161,12 +175,12 @@
         @pl.when(listener)
         def _():
             pl.semaphore_wait(barrier, seq - 1)
-            admit(me - 1)
-
-            @pl.when(row == lax.rem(z + 1, seq // plane))
-            def _():
-                admit(z * (plane + 2))
-                admit(z * (plane + 2) + 1)
+
+            def tell(r, carry):
+                admit(in_half(r))
+                return carry
+
+            lax.fori_loop(1, seq // 2, tell, 0)
 
         @pl.when(jnp.logical_not(listener))
         def _():
@@ -204,19 +218,17 @@
                 pltpu.make_async_copy(other, other, gain_recv.at[which]).wait()
 
             def hand_on(r, carry):
-                step = lax.rem(r + 1, plane)
-                peer = lax.rem(me - 1 + step % 2 + step // 2 * plane, seq)
                 pltpu.make_async_remote_copy(
                     src_ref=gathered,
                     dst_ref=gathered,
                     send_sem=hand_send.at[r],
                     recv_sem=hand_recv,
-                    device_id={"seq": peer},
+                    device_id={"seq": in_half(r)},
                     device_id_type=MESH,
                 ).start()
                 return carry
 
-            lax.fori_loop(1, seq // plane * 2, hand_on, 0)
+            lax.fori_loop(1, seq // 2, hand_on, 0)
 
         def send(clip, slot):
             def one(r, carry):
@@ -224,7 +236,7 @@
                 if slot in (V, DV):
                     to = head % plane // 2
                     told = jnp.logical_or(to == 2 - 2 * half, to == 2 - half)
-                    sent = jnp.logical_and(core == 0, jnp.logical_and(head // plane == row, told))
+                    sent = jnp.logical_and(common, jnp.logical_and(head // plane == row, told))
                     pl.when(jnp.logical_not(sent))(lambda: send_one(clip, slot, head))
                 else:
                     send_one(clip, slot, head)
@@ -292,8 +304,11 @@
             normalize(clip, Q, 0)
 
         def tile_of(i):
-            crosses = i % 2
-            return lax.rem(row + i // 2 + 1, tiles // 2) * 2 + (half + crosses) % 2
+            crosses, k = i % 2, i // 2
+            outer = 1 - (row + 1) // 2 % 2
+            served = k + (1 - outer) * (1 - 2 * (k % 2))
+            near = lax.rem(row + k + 1, tiles // 2)
+            return (crosses * served + (1 - crosses) * near) * 2 + (half + crosses) % 2
 
         def compute(clip, i):
             first = tile_of(i) * per_tile
@@ -399,7 +414,7 @@
                 pltpu.make_async_copy(gathered, gathered, hand_send.at[r]).wait()
                 return carry
 
-            lax.fori_loop(1, seq // plane * 2, handed, 0)
+            lax.fori_loop(1, seq // 2, handed, 0)
 
         for clip in range(clips):
             for slot in range(6):
@@ -436,7 +451,7 @@
                 pltpu.SemaphoreType.DMA((6,)),
                 pltpu.SemaphoreType.DMA((2,)),
                 pltpu.SemaphoreType.DMA((2,)),
-                pltpu.SemaphoreType.DMA((8,)),
+                pltpu.SemaphoreType.DMA((seq // 2,)),
                 pltpu.SemaphoreType.DMA,
                 pltpu.SemaphoreType.REGULAR,
                 pltpu.SemaphoreType.DMA((clips, 6)),

time: 189 us -> 187 us (0.989)
  Pallas kernels: 188 us -> 186 us
where the time goes in v6:
time: 187 us
  Pallas kernels  186 us (99%)
    pallas_call x1, Pallas kernels, on_device(): pl.pallas_call(make_kernel(seq, dp, clips, rows, width), out_shape=(pltpu...  185 us

profile of v6, /device:TPU:37, one launch (start us, length us, event | category | flops | bytes accessed | tf_op | source)
XLA Modules:
  0.0 186.9 jit_solution(5817114214788928194)
XLA Ops:
  0.6 185.0 %shard_map.95 = (bf16[2,64,4096]{2,1,0:T(8,128)(2,1)S(1)}, bf16[2,64,4096]{2,1,0:T(8,128)(2,1)S(1)}) custom-call(bf16[2,64,4096]{2,1,0:T(8,128)(2,1)} %q_ref.1, bf16[2,64,4096]{2,1,0:T(8,128)(2,1)} %k_ref.1, bf16[2,64,4096]{2,1,0:T(8,128)(2,1)} %v_ref.1, bf16[2,64,4096]{2,1,0:T(8,128)(2,1)} %dq_ref.1, bf16[2,64,4096]{2,1,0:T(8,128)(2,1)} %dk_ref.1, ...), custom_call_target="tpu_custom_call" | custom-call | flops 12884901888 | bytes 8388608 | tf_op jit(solution)/shard_map/pallas_call | solution.py:440
  185.6 1.3 shard_map.96

commit v7 on v6

--- a/solution.py
+++ b/solution.py
@@ -306,8 +306,8 @@
         def tile_of(i):
             crosses, k = i % 2, i // 2
             outer = 1 - (row + 1) // 2 % 2
-            served = k + (1 - outer) * (1 - 2 * (k % 2))
             near = lax.rem(row + k + 1, tiles // 2)
+            served = outer * k + (1 - outer) * near
             return (crosses * served + (1 - crosses) * near) * 2 + (half + crosses) % 2
 
         def compute(clip, i):
@@ -384,19 +384,21 @@
         arrive(1, DQ)
         loop(0, tiles, lambda i: give_back(0, 1, i))
 
+        inner = jnp.logical_or(z == 1, z == 2)
+
         def last(i):
             compute(1, i)
             for which in range(2):
                 give_back(1, which, i, range(per_tile // 2))
 
-            @pl.when(jnp.logical_or(half == 0, i % 2 == 0))
+            @pl.when(jnp.logical_or(inner, i % 2 == 0))
             def _():
                 for which in range(2):
                     give_back(1, which, i, range(per_tile // 2, per_tile))
 
         loop(0, tiles, last)
 
-        @pl.when(half == 1)
+        @pl.when(jnp.logical_not(inner))
         def _():
             def rest(i):
                 for which in range(2):

time: 187 us -> 187 us (level)
  Pallas kernels: 186 us -> 184 us
where the time goes in v7:
time: 187 us; the launch traced here: 185 us
  Pallas kernels  184 us (98%)
    pallas_call x1, Pallas kernels, on_device(): pl.pallas_call(make_kernel(seq, dp, clips, rows, width), out_shape=(pltpu...  183 us

profile of v7, /device:TPU:37, one launch (start us, length us, event | category | flops | bytes accessed | tf_op | source)
XLA Modules:
  0.0 185.1 jit_solution(8914423795597083862)
XLA Ops:
  0.6 183.1 %shard_map.95 = (bf16[2,64,4096]{2,1,0:T(8,128)(2,1)S(1)}, bf16[2,64,4096]{2,1,0:T(8,128)(2,1)S(1)}) custom-call(bf16[2,64,4096]{2,1,0:T(8,128)(2,1)} %q_ref.1, bf16[2,64,4096]{2,1,0:T(8,128)(2,1)} %k_ref.1, bf16[2,64,4096]{2,1,0:T(8,128)(2,1)} %v_ref.1, bf16[2,64,4096]{2,1,0:T(8,128)(2,1)} %dq_ref.1, bf16[2,64,4096]{2,1,0:T(8,128)(2,1)} %dk_ref.1, ...), custom_call_target="tpu_custom_call" | custom-call | flops 12884901888 | bytes 8388608 | tf_op jit(solution)/shard_map/pallas_call | solution.py:442
  183.8 1.3 shard_map.96

commit v8 on v6

--- a/solution.py
+++ b/solution.py
@@ -126,17 +126,15 @@
         def _():
             lax.fori_loop(1, dp, greet_dp, 0)
 
-        def source(clip, slot, head):
+        def source(clip, slot, head, early=False):
             columns = pl.ds(pl.multiple_of(head * DIM, DIM), DIM)
-            if slot == V:
-                return v_ref.at[clip, :, columns]
-            if slot == DV:
-                return dv_ref.at[clip, :, columns]
-            return normed.at[slot - K, clip, :, columns]
-
-        def send_one(clip, slot, head):
+            if early:
+                return (v_ref, dv_ref)[slot].at[clip, :, columns]
+            return normed.at[slot, clip, :, columns]
+
+        def send_one(clip, slot, head, early=False):
             pltpu.make_async_remote_copy(
-                src_ref=source(clip, slot, head),
+                src_ref=source(clip, slot, head, early),
                 dst_ref=held.at[clip, slot, me],
                 send_sem=send_sem.at[clip, slot],
                 recv_sem=recv_sem.at[clip, slot],
@@ -148,7 +146,7 @@
             for clip in range(clips):
                 for slot in (V, DV):
                     for k in range(2):
-                        send_one(clip, slot, row * plane + to * 2 + k)
+                        send_one(clip, slot, row * plane + to * 2 + k, early=True)
 
         @pl.when(jnp.logical_and(common, half == 0))
         def _():
@@ -161,9 +159,9 @@
             send_early(0)
             send_early(1)
 
-        sources = {K: k_ref, DK: dk_ref, Q: q_ref, DQ: dq_ref}
+        sources = {V: v_ref, DV: dv_ref, K: k_ref, DK: dk_ref, Q: q_ref, DQ: dq_ref}
         loads = [
-            pltpu.make_async_copy(ref, normed.at[slot - K], load_sem.at[slot - K])
+            pltpu.make_async_copy(ref, normed.at[slot], load_sem.at[slot])
             for slot, ref in sources.items()
         ]
         for copy in loads:
@@ -187,7 +185,7 @@
             pl.semaphore_wait(entered, 1)
 
         gain_loads = [
-            pltpu.make_async_copy(ref, gathered.at[which, group], load_sem.at[4 + which])
+            pltpu.make_async_copy(ref, gathered.at[which, group], load_sem.at[6 + which])
             for which, ref in enumerate((gq_ref, gk_ref))
         ]
 
@@ -261,19 +259,21 @@
         def normalize(clip, slot, which):
             def step(i, carry):
                 part = pl.ds(pl.multiple_of(i * 16, 16), 16)
-                x = normed[slot - K, clip, part, :].astype(jnp.float32)
-                dx = normed[slot + 1 - K, clip, part, :].astype(jnp.float32)
+                x = normed[slot, clip, part, :].astype(jnp.float32)
+                dx = normed[slot + 1, clip, part, :].astype(jnp.float32)
                 gain = gains[which]
                 inverse = lax.rsqrt(jnp.sum(x * x, axis=-1, keepdims=True) * (1.0 / width) + EPS)
                 cross = jnp.sum(x * dx, axis=-1, keepdims=True) * (1.0 / width)
-                normed[slot - K, clip, part, :] = (x * inverse * gain).astype(jnp.bfloat16)
-                normed[slot + 1 - K, clip, part, :] = (
+                normed[slot, clip, part, :] = (x * inverse * gain).astype(jnp.bfloat16)
+                normed[slot + 1, clip, part, :] = (
                     (dx * inverse - x * (inverse * inverse * inverse * cross)) * gain
                 ).astype(jnp.bfloat16)
                 return carry
 
             lax.fori_loop(0, rows // 16, step, 0)
 
+        loads[V].wait()
+        loads[DV].wait()
         send(0, V)
         pl.when(gate)(send_gains)
         send(0, DV)
@@ -292,7 +292,7 @@
                 for j in range(chunks):
                     at = (owner * chunks + j) * DIM
                     gains[which, :, at : at + DIM] = gathered[which, owner, j : j + 1, :]
-        for copy in loads:
+        for copy in loads[K:]:
             copy.wait()
 
         normalize(0, K, 1)
@@ -443,12 +443,12 @@
             in_specs=[pl.BlockSpec(memory_space=pl.ANY)] * 8,
             out_specs=(pl.BlockSpec(memory_space=pltpu.VMEM),) * 2,
             scratch_shapes=[
-                pltpu.VMEM((4, clips, rows, width), jnp.bfloat16),
+                pltpu.VMEM((6, clips, rows, width), jnp.bfloat16),
                 pltpu.VMEM((2, dp) + gq.shape, jnp.float32),
                 pltpu.VMEM((2, 1, width), jnp.float32),
                 pltpu.VMEM((clips, 6, seq, rows, DIM), jnp.bfloat16),
                 pltpu.VMEM((clips, 2, seq, rows, DIM), jnp.bfloat16),
-                pltpu.SemaphoreType.DMA((6,)),
+                pltpu.SemaphoreType.DMA((8,)),
                 pltpu.SemaphoreType.DMA((2,)),
                 pltpu.SemaphoreType.DMA((2,)),
                 pltpu.SemaphoreType.DMA((seq // 2,)),

time: 187 us -> 188 us (level)
  no operation moved by 1% of the time
where the time goes in v8:
time: 188 us; the launch traced here: 187 us
  Pallas kernels  186 us (99%)
    pallas_call x1, Pallas kernels, on_device(): pl.pallas_call(make_kernel(seq, dp, clips, rows, width), out_shape=(pltpu...  185 us

profile of v8, /device:TPU:37, one launch (start us, length us, event | category | flops | bytes accessed | tf_op | source)
XLA Modules:
  0.0 187.0 jit_solution(12868582755671581570)
XLA Ops:
  0.6 185.0 %shard_map.95 = (bf16[2,64,4096]{2,1,0:T(8,128)(2,1)S(1)}, bf16[2,64,4096]{2,1,0:T(8,128)(2,1)S(1)}) custom-call(bf16[2,64,4096]{2,1,0:T(8,128)(2,1)} %q_ref.1, bf16[2,64,4096]{2,1,0:T(8,128)(2,1)} %k_ref.1, bf16[2,64,4096]{2,1,0:T(8,128)(2,1)} %v_ref.1, bf16[2,64,4096]{2,1,0:T(8,128)(2,1)} %dq_ref.1, bf16[2,64,4096]{2,1,0:T(8,128)(2,1)} %dk_ref.1, ...), custom_call_target="tpu_custom_call" | custom-call | flops 12884901888 | bytes 8388608 | tf_op jit(solution)/shard_map/pallas_call | solution.py:440
  185.6 1.3 shard_map.96
